TPU v7x, 128 devices: a whole 4x4x4 slice. The times are simulated.
128 devices in a mesh: gx: 2 (over y_lo), vy: 16 (over z, y_hi, core), vx: 4 (over x).
Axes of the slice: x: 4, y: 4 (y_hi: 2, y_lo: 2; y = y_hi * 2 + y_lo), z: 4, core: 2. Of those that a mesh axis runs over, the one named last changes fastest.
Arguments:
- populations: float32 [32, 32, 32, 2048], P('vy', 'vx', None, 'gx'), may hold values from 0 to 15, as said below
Outputs:
- advanced: float32 [32, 32, 32, 2048], P('vy', 'vx', None, 'gx')
Inputs may be any that keep to these rules, and one draw needn't show every extreme that they name: `populations`: every entry is positive.
All inputs are finite; a program needn't handle non-finite values.
Results may differ from a plain program's by a relative error of at most 0.0003.
Values sent between devices are 32-bit elements; how exact they have to be, the bound alone decides.
A program may use at most 64 MiB of HBM per device.

v0:
```python
import math

import jax
import jax.numpy as jnp
from jax import lax
from jax.sharding import PartitionSpec as P

STEPS = 2


speed_limit = 4.0
marching_delta = 0.125
inverse_relax_period = 16.0
viscous_conductive_ratio = 2.0 / 3.0
thermal_floor = 1.0


def extended(cells, sides, width):
    for axis, dim in sides:
        count = lax.axis_size(axis)
        head = lax.slice_in_dim(cells, 0, width, axis=dim)
        tail = lax.slice_in_dim(cells, cells.shape[dim] - width, cells.shape[dim], axis=dim)
        cells = jnp.concatenate(
            [
                lax.ppermute(tail, axis, [(i, (i + 1) % count) for i in range(count)]),
                cells,
                lax.ppermute(head, axis, [((i + 1) % count, i) for i in range(count)]),
            ],
            axis=dim,
        )
    return cells


def partner_2(x, axis, stride):
    return lax.ppermute(x, axis, [(i, i ^ 1 << stride) for i in range(lax.axis_size(axis))])


def grid_speeds(count):
    spacing = 2.0 * speed_limit / count
    return -speed_limit + (jnp.arange(count, dtype=jnp.float32) + 0.5) * spacing


def upwind(padded, courant, along_dim, length):
    pieces = [
        lax.slice_in_dim(padded, offset, offset + length, axis=along_dim) for offset in range(5)
    ]
    minus_two, minus_one, centre, plus_one, plus_two = pieces
    third = jnp.where(
        courant > 0,
        plus_one - 3.0 * centre + 3.0 * minus_one - minus_two,
        -(minus_one - 3.0 * centre + 3.0 * plus_one - plus_two),
    )
    return (
        centre
        - 0.5 * courant * (plus_one - minus_one)
        + 0.5 * courant * courant * (plus_one - 2.0 * centre + minus_one)
        - courant * (1.0 - courant * courant) / 6.0 * third
    )


def moment_table(speeds_y, speeds_x, weight):
    along_y = speeds_y[:, None]
    along_x = speeds_x[None, :]
    square = along_x * along_x + along_y * along_y
    filler = jnp.ones_like(square)
    table = jnp.stack(
        [
            filler,
            along_x * filler,
            along_y * filler,
            along_x * along_x * filler,
            along_x * along_y,
            along_y * along_y * filler,
            along_x * square,
            along_y * square,
        ]
    )
    return table * weight


def moment_sums(table, swept):
    flat_table = table.reshape(table.shape[0], table.shape[1] * table.shape[2])
    flat_data = swept.reshape(swept.shape[0] * swept.shape[1], swept.shape[2] * swept.shape[3])
    result = jnp.dot(
        flat_table, flat_data, precision=lax.Precision.HIGHEST, preferred_element_type=jnp.float32
    )
    return result.reshape(table.shape[0], swept.shape[2], swept.shape[3])


def equilibrium_parts(sums):
    local_rho_value = sums[0]
    mean_flow_abscissa = sums[1] / local_rho_value
    mean_flow_ordinate = sums[2] / local_rho_value
    kinetic_content_sum = sums[3] + sums[5]
    lattice_norm_sq = (
        mean_flow_abscissa * mean_flow_abscissa + mean_flow_ordinate * mean_flow_ordinate
    )
    thermal_level = jnp.maximum(
        kinetic_content_sum / local_rho_value - lattice_norm_sq, thermal_floor
    )
    conduction_abscissa = 0.5 * (
        sums[6]
        - 2.0 * (mean_flow_abscissa * sums[3] + mean_flow_ordinate * sums[4])
        - mean_flow_abscissa * kinetic_content_sum
        + 2.0 * local_rho_value * lattice_norm_sq * mean_flow_abscissa
    )
    conduction_ordinate = 0.5 * (
        sums[7]
        - 2.0 * (mean_flow_abscissa * sums[4] + mean_flow_ordinate * sums[5])
        - mean_flow_ordinate * kinetic_content_sum
        + 2.0 * local_rho_value * lattice_norm_sq * mean_flow_ordinate
    )
    return (
        local_rho_value,
        mean_flow_abscissa,
        mean_flow_ordinate,
        thermal_level,
        conduction_abscissa,
        conduction_ordinate,
    )


def relax(read, along_y, along_x, macroscopic_quantities):
    (
        local_rho_value,
        mean_flow_abscissa,
        mean_flow_ordinate,
        thermal_level,
        conduction_abscissa,
        conduction_ordinate,
    ) = macroscopic_quantities
    peculiar_abscissa = along_x - mean_flow_abscissa
    peculiar_ordinate = along_y - mean_flow_ordinate
    peculiar_norm_sq = peculiar_abscissa * peculiar_abscissa + peculiar_ordinate * peculiar_ordinate
    gaussian_equilibrium = (
        local_rho_value / (math.pi * thermal_level) * jnp.exp(-peculiar_norm_sq / thermal_level)
    )
    corrected_equilibrium = gaussian_equilibrium * (
        1.0
        + 4.0
        * (1.0 - viscous_conductive_ratio)
        * (conduction_abscissa * peculiar_abscissa + conduction_ordinate * peculiar_ordinate)
        / (local_rho_value * thermal_level * thermal_level)
        * (peculiar_norm_sq / thermal_level - 2.0)
    )
    retain_mask = jnp.exp(
        -marching_delta * local_rho_value * jnp.sqrt(thermal_level) / inverse_relax_period
    )
    return corrected_equilibrium + (read - corrected_equilibrium) * retain_mask


def advance_once(current, speeds_y, speeds_x, table):
    rows = current.shape[2]
    cells = current.shape[3]
    groups_y = lax.axis_size("vy")
    wrapped = extended(current, (("gx", 3),), 2)
    swept = upwind(wrapped, marching_delta * speeds_x[None, :, None, None], 3, cells)
    strip = jnp.concatenate([swept[:, :, 0:2], swept[:, :, rows - 2 : rows]], axis=2)
    partner = strip
    for bit_number in range(groups_y.bit_length() - 1):
        partner = partner_2(partner, "vy", bit_number)
    mirrored = jnp.flip(partner, 0)
    lower = jnp.flip(mirrored[:, :, 0:2], 2)
    upper = jnp.flip(mirrored[:, :, 2:4], 2)
    walled = jnp.concatenate([lower, swept, upper], axis=2)
    swept = upwind(walled, marching_delta * speeds_y[:, None, None, None], 2, rows)
    sums = moment_sums(table, swept)
    totals = lax.psum(sums, ("vy", "vx"))
    macroscopic_quantities = equilibrium_parts(totals)
    return relax(
        swept, speeds_y[:, None, None, None], speeds_x[None, :, None, None], macroscopic_quantities
    )


def on_device(populations):
    local_y = populations.shape[0]
    local_x = populations.shape[1]
    count_y = local_y * lax.axis_size("vy")
    count_x = local_x * lax.axis_size("vx")
    speeds_y = lax.dynamic_slice_in_dim(
        grid_speeds(count_y), lax.axis_index("vy") * local_y, local_y
    )
    speeds_x = lax.dynamic_slice_in_dim(
        grid_speeds(count_x), lax.axis_index("vx") * local_x, local_x
    )
    weight = 2.0 * speed_limit / count_y * (2.0 * speed_limit / count_x)
    table = moment_table(speeds_y, speeds_x, weight)
    current = populations
    for step_index in range(STEPS):
        current = advance_once(current, speeds_y, speeds_x, table)
    return current


def solution(mesh):
    return jax.shard_map(
        on_device,
        mesh=mesh,
        in_specs=(P("vy", "vx", None, "gx"),),
        out_specs=P("vy", "vx", None, "gx"),
        check_vma=False,
    )
```

profile of v0, /device:TPU:1, one launch (start us, length us, event | category | flops | bytes accessed | tf_op | source)
XLA Modules:
  0.0 1415.6 jit_solution(1995879202879966264)
XLA Ops:
  6.5 1.2 fusion.88
  7.7 2.2 collective-permute-start
  10.1 1.9 constant_dynamic-update-slice_fusion.1
  12.0 3.5 collective-permute-done
  15.6 5.6 collective-permute-done.1
  21.1 2.6 fusion.48
  23.8 1.3 copy-done.1
  25.2 0.1 pad_maximum_fusion.7
  25.4 1.7 collective-permute-start.2
  27.1 1.2 collective-permute-done.2
  28.2 3.1 collective-permute-start.3
  31.3 6.2 collective-permute-done.3
  37.5 1.6 collective-permute-start.4
  39.6 4.8 collective-permute-done.4
  44.4 3.2 collective-permute-start.5
  48.0 4.9 collective-permute-done.5
  52.9 0.5 rev.16
  53.4 0.5 rev.17
  53.9 7.0 fusion.43
  61.0 3.2 fusion.24
  64.2 639.5 %all-reduce.3.cloned.1.call-done = f32[8,32,1024]{2,0,1:T(8,128)} async-done(((f32[8,32,1024]{2,0,1:T(8,128)}), f32[8,32,1024]{2,0,1:T(8,128)}) %all-reduce.3.cloned.1.call-update) | async-done | bytes 1048592 | tf_op jit(solution)/shard_map/psum | solution.py:168
  703.8 6.0 fusion.89
  709.8 0.3 fusion.63
  710.1 0.3 subtract_multiply_fusion.3
  710.6 1.2 multiply_add_fusion.1
  711.8 0.1 fusion.86
  711.9 0.4 collective-permute-start.6
  712.4 1.1 collective-permute-start.7
  713.5 3.8 collective-permute-done.6
  717.2 4.1 collective-permute-done.7
  721.3 3.0 fusion.37
  724.4 1.3 copy-done.2
  725.8 0.1 pad_maximum_fusion.8
  726.0 5.1 collective-permute-start.8
  731.0 1.2 collective-permute-done.8
  732.2 9.0 collective-permute-done.9
  741.2 6.6 collective-permute-done.10
  747.8 7.1 collective-permute-done.11
  755.0 0.5 rev.18
  755.5 0.5 rev.19
  756.0 7.0 fusion.31
  763.0 2.2 fusion.21
  765.2 1.6 copy.19
  766.9 636.4 %all-reduce.5.cloned.1.call-done = f32[8,32,1024]{2,1,0:T(8,128)} async-done(((f32[8,32,1024]{2,1,0:T(8,128)}), f32[8,32,1024]{2,1,0:T(8,128)}) %all-reduce.5.cloned.1.call-update) | async-done | bytes 1048592 | tf_op jit(solution)/shard_map/psum | solution.py:168
  1403.2 1.2 multiply_divide_fusion
  1404.5 1.4 fusion.57
  1405.8 0.3 subtract_multiply_fusion.1
  1406.3 2.5 multiply_add_fusion
  (42 shorter events, 1.9 us)
Async XLA Ops:
  6.5 697.2 %all-reduce.3.cloned.1.call-start = ((), (), s32[]{:S(2)}) async-start(), calls=%async_computation | async-start | bytes 2097152 | tf_op jit(solution)/shard_map/psum | solution.py:168
  7.7 7.8 collective-permute-start
  9.9 11.2 collective-permute-start.1
  10.1 11.0 copy-start
  23.8 1.3 copy-start.1
  25.4 2.9 collective-permute-start.2
  28.2 9.3 collective-permute-start.3
  37.5 6.9 collective-permute-start.4
  44.4 8.4 collective-permute-start.5
  64.2 1339.0 %all-reduce.5.cloned.1.call-start = ((), (), s32[]{:S(2)}) async-start(), calls=%async_computation.1 | async-start | bytes 2097152 | tf_op jit(solution)/shard_map/psum | solution.py:168
  711.9 5.3 collective-permute-start.6
  712.4 9.0 collective-permute-start.7
  724.4 1.3 copy-start.2
  726.0 6.2 collective-permute-start.8
  732.2 9.0 collective-permute-start.9
  741.2 6.6 collective-permute-start.10
  747.8 7.1 collective-permute-start.11
Sparse Core Ops, SparseCore 0:
  64.3 639.3 all-reduce.2
  767.0 636.2 all-reduce.4
where the time goes:
time: 1420 us
  waiting for transfers between devices  1330 us (94%)
  other arithmetic  27.7 us (2%)
  starting transfers between devices  18.5 us (1%)
  local copies, waits for them, and re-layouts  16.6 us (1%)
    psum x2, waiting for transfers between devices, advance_once(): totals = lax.psum(sums, ('vy', 'vx'))  1280 us
    ppermute x8, waiting for transfers between devices, partner_2(): lax.ppermute(x, axis, [(i, i ^ 1 << stride) for i in range(lax.axis_size(...  40.8 us
  transfers between devices with their start and end apart: 14, of which 14 were waited for; matrix products, arithmetic and copies ran while one was open for 0% of the time, Pallas kernels for 0%

commit v1 on v0

v1 whole, which is shorter than its diff:
```python
import math

import jax
import jax.numpy as jnp
from jax import lax
from jax.experimental import pallas as pl
from jax.experimental.pallas import tpu as pltpu
from jax.sharding import PartitionSpec as P

STEPS = 2
DT = 0.125
TAU0 = 16.0
PRANDTL = 2.0 / 3.0
FLOOR = 1.0
MESH = pl.DeviceIdType.MESH
F32 = jnp.float32

LY, LX, ROWS, CHUNKS, TILES = 2, 8, 32, 8, 4
LV = LY * LX
PAD = 48
CHIPS = 32


def speed(index):
    return (index.astype(F32) + 0.5) * 0.25 - 4.0


def taps(nu):
    a = jnp.abs(nu)
    e = a * (1.0 - a * a) * (1.0 / 6.0)
    h = 0.5 * a
    s = 0.5 * a * a
    return 1.0 - 2.0 * s + 3.0 * e, h + s - 3.0 * e, e, s - h - e


def total_wait(ref, sem):
    pltpu.make_async_copy(ref, ref, sem).wait()


def kernel(
    x_hbm, o_hbm, A, G, HS, HR, WS, WR, MO, R1, S, R2, T4, FO, FB,
    in_sem, out_sem, h_sem, w_sem, c_sem, rs_sem, ag_sem, d_sem,
):
    g, v, x = lax.axis_index("gx"), lax.axis_index("vy"), lax.axis_index("vx")
    z, yh, c = v // 4, (v // 2) % 2, v % 2
    other = 1 - c
    q_me = (x * 4 + z) * 2 + yh
    core_dev = (g, v + 1 - 2 * c, x)
    gx_dev = (1 - g, v, x)
    mirror_dev = (g, 15 - v, x)

    def chip(d):
        xx, zz, yy = (x + d // 8) % 4, (z + (d // 2) % 4) % 4, (yh + d % 2) % 2
        return (g, zz * 4 + yy * 2 + c, xx), (xx * 4 + zz) * 2 + yy

    barrier = pltpu.get_barrier_semaphore()

    def load(k):
        return pltpu.make_async_copy(
            x_hbm.at[:, :, pl.ds(k * 128, 128)], A.at[:, k], in_sem.at[k]
        )

    for k in range(CHUNKS):
        load(k).start()
    for d in (core_dev, gx_dev, mirror_dev):
        pl.semaphore_signal(barrier, inc=1, device_id=d, device_id_type=MESH)

    @pl.loop(1, CHIPS)
    def _(d):
        pl.semaphore_signal(barrier, inc=1, device_id=chip(d)[0], device_id_type=MESH)

    for k in range(CHUNKS):
        load(k).wait()
    pl.semaphore_wait(barrier, CHIPS - 1 + 3)

    lane = lax.broadcasted_iota(jnp.int32, (8, 128), 1)
    right = x >= 2
    up = v >= 8
    sx = jnp.where(right, 1, -1)
    kx0 = jnp.where(right, 0, 7)
    roll_u1 = jnp.where(right, 1, 127)
    roll_u2 = jnp.where(right, 2, 126)
    roll_d1 = jnp.where(right, 127, 1)
    edge = jnp.where(right, lane, 127 - lane)
    m_u1, m_u2, m_d1 = edge < 1, edge < 2, edge > 126
    sy = jnp.where(up, 1, -1)
    ghost0 = jnp.where(up, 0, 1)
    cx0 = x * LX
    cy = [speed(v * LY + j) for j in range(LY)]
    cy_taps = [taps(DT * s) for s in cy]
    mid = speed(cx0 + 3) + 0.125

    def step(n, _):
        HS[n] = jnp.zeros((2, 8, 128), F32)

        @pl.loop(0, LV)
        def _(ji):
            acc = jnp.zeros((8, 128), F32)
            for t in range(TILES):
                rows = pl.ds(8 * t, 8)
                head = pltpu.roll(A[ji, 0, rows, :], 4 * t, 1)
                tail = pltpu.roll(A[ji, 7, rows, :], (4 * t + 4) % 128, 1)
                acc = jnp.where((lane >= 4 * t) & (lane < 4 * t + 2), head, acc)
                acc = jnp.where((lane >= 4 * t + 2) & (lane < 4 * t + 4), tail, acc)
            HS[n, ji // 8] = HS[n, ji // 8] + pltpu.roll(acc, 16 * (ji % 8), 1)

        halo = pltpu.make_async_remote_copy(
            src_ref=HS.at[n], dst_ref=HR.at[n], send_sem=h_sem.at[n, 0], recv_sem=h_sem.at[n, 1],
            device_id=gx_dev, device_id_type=MESH,
        )
        halo.start()
        halo.wait()

        @pl.loop(0, LV * TILES)
        def _(it):
            ji, t = it // TILES, it % TILES
            rows = pl.ds(pl.multiple_of(8 * t, 8), 8)
            c0, c1, c2, c3 = taps(DT * speed(cx0 + ji % LX))
            ends = HR[n, ji // 8]
            base = 16 * (ji % 8) + 4 * t
            from_left = (252 - base) % 128
            from_right = (128 - base) % 128
            ext = [pltpu.roll(ends, jnp.where(right, from_left, from_right), 1)]
            where = [kx0 + sx * k for k in range(CHUNKS)]
            ext += [A[ji, k, rows, :] for k in where]
            ext += [pltpu.roll(ends, jnp.where(right, from_right, from_left), 1)]
            ru1 = [pltpu.roll(e, roll_u1, 1) for e in ext[:9]]
            ru2 = [pltpu.roll(e, roll_u2, 1) for e in ext[:9]]
            rd1 = [pltpu.roll(e, roll_d1, 1) for e in ext[1:]]
            for k in range(CHUNKS):
                u1 = jnp.where(m_u1, ru1[k], ru1[k + 1])
                u2 = jnp.where(m_u2, ru2[k], ru2[k + 1])
                d1 = jnp.where(m_d1, rd1[k + 1], rd1[k])
                out = (c0 * ext[k + 1] + c1 * u1) + (c2 * u2 + c3 * d1)
                G[ji, pl.ds(pl.multiple_of(where[k] * PAD + 8 + 8 * t, 8), 8), :] = out

        @pl.loop(0, 4 * LV)
        def _(it):
            r, ji = it // LV, it % LV
            row = jnp.where(r < 2, 1 - r, 33 - r) + 8
            WS[n, r, ji] = G[ji, pl.ds(row, 8, stride=PAD), :]

        send0 = 1 - ghost0
        mirror = pltpu.make_async_remote_copy(
            src_ref=WS.at[n, pl.ds(send0, 3)], dst_ref=WR.at[n, pl.ds(send0, 3)],
            send_sem=w_sem.at[n, 0], recv_sem=w_sem.at[n, 1],
            device_id=mirror_dev, device_id_type=MESH,
        )
        mirror.start()
        mirror.wait()

        @pl.loop(0, 3 * LV)
        def _(it):
            r, ji = it // LV + ghost0, it % LV
            row = jnp.where(r < 2, 6 + r, 38 + r)
            G[ji, pl.ds(row, 8, stride=PAD), :] = WR[n, r, (ji + 8) % 16]

        @pl.loop(0, TILES * CHUNKS)
        def _(it):
            t, k = it // CHUNKS, it % CHUNKS
            b = k * PAD + 8 + 8 * t
            rows = pl.ds(pl.multiple_of(8 * t, 8), 8)
            M = []
            for j in range(LY):
                c0, c1, c2, c3 = cy_taps[j]
                r = []
                for i in range(LX):
                    ji = j * LX + i
                    val = (
                        c0 * G[ji, pl.ds(b, 8), :] + c1 * G[ji, pl.ds(b - sy, 8), :]
                    ) + (c2 * G[ji, pl.ds(b - 2 * sy, 8), :] + c3 * G[ji, pl.ds(b + sy, 8), :])
                    A[ji, k, rows, :] = val
                    r.append(val)
                p = [r[4 + i] + r[3 - i] for i in range(4)]
                d = [r[4 + i] - r[3 - i] for i in range(4)]
                s = [0.125 + 0.25 * i for i in range(4)]
                L0 = (p[0] + p[1]) + (p[2] + p[3])
                L1 = (s[0] * d[0] + s[1] * d[1]) + (s[2] * d[2] + s[3] * d[3])
                L2 = (s[0] ** 2 * p[0] + s[1] ** 2 * p[1]) + (s[2] ** 2 * p[2] + s[3] ** 2 * p[3])
                L3 = (s[0] ** 3 * d[0] + s[1] ** 3 * d[1]) + (s[2] ** 3 * d[2] + s[3] ** 3 * d[3])
                M1 = L1 + mid * L0
                M2 = L2 + mid * (L1 + M1)
                M3 = L3 + mid * (3.0 * L2 + mid * (3.0 * L1 + mid * L0))
                M.append((L0, M1, M2, M3))
            (a0, a1, a2, a3), (b0, b1, b2, b3) = M
            ya, yb = cy
            ya0, yb0 = ya * a0, yb * b0
            ya1, yb1 = ya * a1, yb * b1
            sums = [
                a0 + b0,
                a1 + b1,
                ya0 + yb0,
                a2 + b2,
                ya1 + yb1,
                ya * ya0 + yb * yb0,
                (a3 + b3) + (ya * ya1 + yb * yb1),
                ya * (a2 + ya * ya0) + yb * (b2 + yb * yb0),
            ]
            for m in range(8):
                MO[n, k // 4, t, k % 4, pl.ds(m, 8, stride=8), :] = sums[m]

        core = pltpu.make_async_remote_copy(
            src_ref=MO.at[n, other], dst_ref=R1.at[n], send_sem=c_sem.at[n, 0], recv_sem=c_sem.at[n, 1],
            device_id=core_dev, device_id_type=MESH,
        )
        core.start()
        core.wait()

        @pl.loop(0, CHIPS)
        def _(q):
            rows = pl.ds(pl.multiple_of((q % 8) * 8, 8), 8)
            for t in range(TILES):
                S[n, q, t] = MO[n, c, t, q // 8, rows, :] + R1[n, t, q // 8, rows, :]

        @pl.loop(1, CHIPS)
        def _(d):
            dev, q = chip(d)
            pltpu.make_async_remote_copy(
                src_ref=S.at[n, q], dst_ref=R2.at[n, d - 1],
                send_sem=rs_sem.at[n, 0], recv_sem=rs_sem.at[n, 1],
                device_id=dev, device_id_type=MESH,
            ).start()

        total_wait(R2.at[n], rs_sem.at[n, 1])
        T4[...] = lax.fori_loop(
            0, CHIPS - 1, lambda d, acc: acc + R2[n, d], S[n, q_me], unroll=True
        ).reshape(TILES * 8, 128)
        s = [T4[pl.ds(m, TILES, stride=8), :] * 0.0625 for m in range(8)]
        rho = s[0]
        inv = 1.0 / rho
        ux, uy = s[1] * inv, s[2] * inv
        energy = s[3] + s[5]
        uu = ux * ux + uy * uy
        temp = jnp.maximum(energy * inv - uu, FLOOR)
        qx = 0.5 * (s[6] - 2.0 * (ux * s[3] + uy * s[4]) - ux * energy + 2.0 * rho * uu * ux)
        qy = 0.5 * (s[7] - 2.0 * (ux * s[4] + uy * s[5]) - uy * energy + 2.0 * rho * uu * uy)
        it = 1.0 / temp
        keep = jnp.exp((-DT / TAU0) * rho * jnp.sqrt(temp))
        scale = (4.0 * (1.0 - PRANDTL)) * inv * it * it
        fields = [ux, uy, it, rho * it * (1.0 / math.pi) * (1.0 - keep), keep, scale * qx, scale * qy, rho]
        for m in range(8):
            FO[n, pl.ds(m, TILES, stride=8), :] = fields[m]
        mine = FO[n]
        FB[n, c, pl.ds(pl.multiple_of(q_me * 32, 32), 32)] = mine

        @pl.loop(1, CHIPS)
        def _(d):
            dev, _q = chip(d)
            pltpu.make_async_remote_copy(
                src_ref=FO.at[n], dst_ref=FB.at[n, c, pl.ds(pl.multiple_of(q_me * 32, 32), 32)],
                send_sem=ag_sem.at[n, 0], recv_sem=ag_sem.at[n, 1],
                device_id=dev, device_id_type=MESH,
            ).start()

        total_wait(FB.at[n, c, pl.ds(0, (CHIPS - 1) * 32)], ag_sem.at[n, 1])
        back = pltpu.make_async_remote_copy(
            src_ref=FB.at[n, c], dst_ref=FB.at[n, c], send_sem=d_sem.at[n, 0], recv_sem=d_sem.at[n, 1],
            device_id=core_dev, device_id_type=MESH,
        )
        back.start()
        total_wait(R2.at[n], rs_sem.at[n, 0])
        total_wait(FB.at[n, c, pl.ds(0, (CHIPS - 1) * 32)], ag_sem.at[n, 0])
        back.wait()

        @pl.loop(0, TILES * CHUNKS)
        def _(it):
            t, k = it // CHUNKS, it % CHUNKS
            rows = pl.ds(pl.multiple_of(8 * t, 8), 8)
            first = (k % 4) * (8 * TILES * 8) + 8 * t
            ux, uy, it_, gp, keep, bx, by = [
                FB[n, k // 4, pl.ds(first + m, 8, stride=TILES * 8), :] for m in range(7)
            ]
            ax, ex, bxi = [], [], []
            for i in range(LX):
                xi = speed(cx0 + i) - ux
                a = xi * xi * it_
                ax.append(a)
                ex.append(jnp.exp(-a))
                bxi.append(bx * xi)
            for j in range(LY):
                yj = cy[j] - uy
                ay = yj * yj * it_
                ey = gp * jnp.exp(-ay)
                ay = ay - 2.0
                bj = by * yj
                for i in range(LX):
                    ji = j * LX + i
                    shakhov = ex[i] * ey * (1.0 + (bxi[i] + bj) * (ax[i] + ay))
                    A[ji, k, rows, :] = A[ji, k, rows, :] * keep + shakhov

        return 0

    lax.fori_loop(0, STEPS, step, 0)

    def store(k):
        return pltpu.make_async_copy(
            A.at[:, k], o_hbm.at[:, :, pl.ds(k * 128, 128)], out_sem.at[k]
        )

    for k in range(CHUNKS):
        store(k).start()
    for k in range(CHUNKS):
        store(k).wait()


def on_device(populations):
    shape = (LV, ROWS, CHUNKS * 128)
    dma = pltpu.SemaphoreType.DMA
    out = pl.pallas_call(
        kernel,
        out_shape=jax.ShapeDtypeStruct(shape, F32),
        in_specs=[pl.BlockSpec(memory_space=pl.ANY)],
        out_specs=pl.BlockSpec(memory_space=pl.ANY),
        scratch_shapes=[
            pltpu.VMEM((LV, CHUNKS, ROWS, 128), F32),
            pltpu.VMEM((LV, CHUNKS * PAD, 128), F32),
            pltpu.VMEM((STEPS, 2, 8, 128), F32),
            pltpu.VMEM((STEPS, 2, 8, 128), F32),
            pltpu.VMEM((STEPS, 4, LV, 8, 128), F32),
            pltpu.VMEM((STEPS, 4, LV, 8, 128), F32),
            pltpu.VMEM((STEPS, 2, TILES, 4, 64, 128), F32),
            pltpu.VMEM((STEPS, TILES, 4, 64, 128), F32),
            pltpu.VMEM((STEPS, CHIPS, TILES, 8, 128), F32),
            pltpu.VMEM((STEPS, CHIPS - 1, TILES, 8, 128), F32),
            pltpu.VMEM((TILES * 8, 128), F32),
            pltpu.VMEM((STEPS, TILES * 8, 128), F32),
            pltpu.VMEM((STEPS, 2, CHIPS * TILES * 8, 128), F32),
            dma((CHUNKS,)),
            dma((CHUNKS,)),
            dma((STEPS, 2)),
            dma((STEPS, 2)),
            dma((STEPS, 2)),
            dma((STEPS, 2)),
            dma((STEPS, 2)),
            dma((STEPS, 2)),
        ],
        compiler_params=pltpu.CompilerParams(
            collective_id=0, has_side_effects=True, vmem_limit_bytes=40 << 20
        ),
        cost_estimate=pl.CostEstimate(flops=60 << 20, bytes_accessed=4 << 20, transcendentals=1 << 20),
    )(populations.reshape(shape))
    return out.reshape(populations.shape)


def solution(mesh):
    return jax.shard_map(
        on_device,
        mesh=mesh,
        in_specs=(P("vy", "vx", None, "gx"),),
        out_specs=P("vy", "vx", None, "gx"),
        check_vma=False,
    )
```

time: 1420 us -> 118 us (0.08)
  waiting for transfers between devices: 1330 us -> 0 us
  Pallas kernels: 0 us -> 115 us
  other arithmetic: 27.7 us -> 0 us
  starting transfers between devices: 18.5 us -> 0 us
    psum x2 -> x0, waiting for transfers between devices: 1280 us -> none  [advance_once(): totals = lax.psum(sums, ('vy', 'vx'))]
    pallas_call x0 -> x1, Pallas kernels: none -> 115 us  [on_device(): pl.pallas_call(kernel, out_shape=jax.ShapeDtypeStruct(shape, F32), in_spe...]
    ppermute x12 -> x0, waiting for transfers between devices: 57.8 us -> none  [the longest x8 40.8 us: partner_2(): lax.ppermute(x, axis, [(i, i ^ 1 << stride) for i in range(lax.axis_size(...]
    sub x4 -> x0, other arithmetic: 19.7 us -> none  [upwind(): centre - 0.5 * courant * (plus_one - minus_one)]
    ppermute x12 -> x0, starting transfers between devices: 18.5 us -> none  [the longest x8 14.6 us: partner_2(): lax.ppermute(x, axis, [(i, i ^ 1 << stride) for i in range(lax.axis_size(...]
  transfers between devices with their start and end apart: 14 -> 0, of which waited for: 14 -> 0; matrix products, arithmetic and copies ran while one was open for 0% -> 0% of each run, Pallas kernels for 0% -> 0%
where the time goes in v1:
time: 118 us
  Pallas kernels  115 us (97%)
  local copies, waits for them, and re-layouts  2.91 us (2%)
    pallas_call x1, Pallas kernels, on_device(): pl.pallas_call(kernel, out_shape=jax.ShapeDtypeStruct(shape, F32), in_spe...  115 us
    unnamed x3, local copies, waits for them, and re-layouts  2.91 us

profile of v1, /device:TPU:1, one launch (start us, length us, event | category | flops | bytes accessed | tf_op | source)
XLA Modules:
  0.0 117.6 jit_solution(2628480677015411288)
XLA Ops:
  0.0 0.0 copy-start
  0.0 1.6 %copy-done = f32[2,8,32,1024]{3,2,1,0:T(8,128)S(1)} copy-done((f32[2,8,32,1024]{3,2,1,0:T(8,128)S(1)}, f32[2,8,32,1024]{3,2,1,0:T(8,128)}, u32[]{:S(2)}) %copy-start) | copy-done | bytes 2097176
  1.6 114.7 %shard_map.17 = f32[16,32,1024]{2,1,0:T(8,128)S(1)} custom-call(f32[16,32,1024]{2,1,0:T(8,128)S(1)} %bitcast.3), custom_call_target="tpu_custom_call" | custom-call | flops 62914560 | bytes 4194304 | tf_op jit(solution)/shard_map/pallas_call | solution.py:309
  116.3 1.3 %copy.3 = f32[2,8,32,1024]{3,2,1,0:T(8,128)} copy(f32[2,8,32,1024]{3,2,1,0:T(8,128)S(1)} %bitcast.2) | data formatting | bytes 4194304
Async XLA Ops:
  0.0 1.6 %copy-start = (f32[2,8,32,1024]{3,2,1,0:T(8,128)S(1)}, f32[2,8,32,1024]{3,2,1,0:T(8,128)}, u32[]{:S(2)}) copy-start(f32[2,8,32,1024]{3,2,1,0:T(8,128)} %param.1) | copy-start | bytes 6291460

commit v2 on v0

v2 whole, which is shorter than its diff:
```python
import math

import jax
import jax.numpy as jnp
from jax import lax
from jax.experimental import pallas as pl
from jax.experimental.pallas import tpu as pltpu
from jax.sharding import PartitionSpec as P

STEPS = 2
DT = 0.125
TAU0 = 16.0
PRANDTL = 2.0 / 3.0
FLOOR = 1.0
MESH = pl.DeviceIdType.MESH
F32 = jnp.float32

LY, LX, ROWS, CHUNKS, TILES = 2, 8, 32, 8, 4
LV = LY * LX
PAD = 48
CHIPS = 32
FAR_FIRST = sorted(
    ((a, b, e) for a in range(4) for b in range(4) for e in range(2) if a or b or e),
    key=lambda t: -(min(t[0], 4 - t[0]) + min(t[1], 4 - t[1]) + 2 * t[2]),
)


def speed(index):
    return (index.astype(F32) + 0.5) * 0.25 - 4.0


def taps(nu):
    a = jnp.abs(nu)
    e = a * (1.0 - a * a) * (1.0 / 6.0)
    h = 0.5 * a
    s = 0.5 * a * a
    return 1.0 - 2.0 * s + 3.0 * e, h + s - 3.0 * e, e, s - h - e


def total_wait(ref, sem):
    pltpu.make_async_copy(ref, ref, sem).wait()


def kernel(
    x_hbm, A, TX, G, HS, HR, HX, MO, R1, S, R2, T4, FO, FB,
    in_sem, h_sem, w_sem, c_sem, rs_sem, ag_sem, d_sem,
):
    g, v, x = lax.axis_index("gx"), lax.axis_index("vy"), lax.axis_index("vx")
    z, yh, c = v // 4, (v // 2) % 2, v % 2
    other = 1 - c
    q_me = (x * 4 + z) * 2 + yh
    core_dev = (g, v + 1 - 2 * c, x)
    gx_dev = (1 - g, v, x)
    mirror_dev = (g, 15 - v, x)
    chips = []
    for dx, dz, dy in FAR_FIRST:
        xx, zz, yy = (x + dx) % 4, (z + dz) % 4, (yh + dy) % 2
        chips.append(((g, zz * 4 + yy * 2 + c, xx), (xx * 4 + zz) * 2 + yy))

    load = pltpu.make_async_copy(x_hbm, A, in_sem)
    load.start()
    barrier = pltpu.get_barrier_semaphore()
    for d in (core_dev, gx_dev, mirror_dev):
        pl.semaphore_signal(barrier, inc=1, device_id=d, device_id_type=MESH)
    for d, _ in chips:
        pl.semaphore_signal(barrier, inc=1, device_id=d, device_id_type=MESH)

    cx0 = x * LX
    for i in range(LX):
        for m, tap in enumerate(taps(DT * speed(cx0 + i))):
            TX[i, m] = tap
    lane = lax.broadcasted_iota(jnp.int32, (8, 128), 1)
    right = x >= 2
    up = v >= 8
    sy = jnp.where(up, 1, -1)
    send0 = jnp.where(up, 1, 0)
    cy = [speed(v * LY + j) for j in range(LY)]
    cy_taps = [taps(DT * s) for s in cy]
    mid = speed(cx0 + 3) + 0.125

    load.wait()
    pl.semaphore_wait(barrier, CHIPS - 1 + 3)

    def tile(group, tt):
        return 1 + tt if group == 0 else 3 * tt

    def block(t, k):
        return pl.ds(pl.multiple_of(8 * t, 8), 8), pl.ds(pl.multiple_of(128 * k, 128), 128)

    def step(n, _):
        for part in range(2):
            acc = jnp.zeros((8, 128), F32)
            for p in range(32):
                ji, t = (part * 32 + p) // TILES, p % TILES
                ends = jnp.where(lane < 64, A[ji, 8 * t : 8 * t + 8, :128], A[ji, 8 * t : 8 * t + 8, 896:])
                ends = pltpu.roll(ends, (4 * p + 2) % 128, 1)
                acc = jnp.where((lane >= 4 * p) & (lane < 4 * p + 4), ends, acc)
            HS[n, part] = acc

        halo = pltpu.make_async_remote_copy(
            src_ref=HS.at[n], dst_ref=HR.at[n], send_sem=h_sem.at[n, 0], recv_sem=h_sem.at[n, 1],
            device_id=gx_dev, device_id_type=MESH,
        )
        halo.start()
        halo.wait()

        for part in range(2):
            ends = HR[n, part]
            for p in range(32):
                HX[part * 32 + p] = pltpu.roll(ends, (126 - 4 * p) % 128, 1)

        def stream(toward_right, tiles):
            order = list(range(CHUNKS)) if toward_right else list(range(CHUNKS - 1, -1, -1))
            edge = lane if toward_right else 127 - lane
            shift = (lambda a: a) if toward_right else (lambda a: 128 - a)
            m_u1, m_u2, m_d1 = edge < 1, edge < 2, edge > 126

            @pl.loop(0, LV)
            def _(ji):
                c0, c1, c2, c3 = [TX[ji % LX, m] for m in range(4)]
                for t in tiles:
                    ends = HX[ji * TILES + t]
                    ext = [ends] + [A[ji, 8 * t : 8 * t + 8, 128 * k : 128 * k + 128] for k in order] + [ends]
                    ru1 = [pltpu.roll(e, shift(1), 1) for e in ext[:9]]
                    ru2 = [pltpu.roll(e, shift(2), 1) for e in ext[:9]]
                    rd1 = [pltpu.roll(e, shift(127), 1) for e in ext[1:]]
                    for k in range(CHUNKS):
                        u1 = jnp.where(m_u1, ru1[k], ru1[k + 1])
                        u2 = jnp.where(m_u2, ru2[k], ru2[k + 1])
                        d1 = jnp.where(m_d1, rd1[k + 1], rd1[k])
                        out = (c0 * ext[k + 1] + c1 * u1) + (c2 * u2 + c3 * d1)
                        G[ji, order[k], pl.ds(8 + 8 * t, 8), :] = out

        def stream_tiles(*tiles):
            pl.when(right)(lambda: stream(True, tiles))
            pl.when(jnp.logical_not(right))(lambda: stream(False, tiles))

        stream_tiles(0, 3)

        mirrors = []
        for j in range(LY):
            for r in range(3):
                row = r + send0
                row = jnp.where(row < 2, 1 - row, 33 - row) + 8
                mirrors.append(pltpu.make_async_remote_copy(
                    src_ref=G.at[pl.ds(j * LX, LX), :, row, :],
                    dst_ref=G.at[pl.ds((1 - j) * LX, LX), :, jnp.where(row < 20, 15 - row, 79 - row), :],
                    send_sem=w_sem.at[n, 0, j * 3 + r], recv_sem=w_sem.at[n, 1, j * 3 + r],
                    device_id=mirror_dev, device_id_type=MESH,
                ))
        for m in mirrors:
            m.start()

        stream_tiles(1, 2)

        def sweep(group):
            @pl.loop(0, 2 * CHUNKS)
            def _(it):
                tt, k = it // CHUNKS, it % CHUNKS
                t = tile(group, tt)
                b = 8 + 8 * t
                rows, cols = block(t, k)
                M = []
                for j in range(LY):
                    c0, c1, c2, c3 = cy_taps[j]
                    r = []
                    for i in range(LX):
                        ji = j * LX + i
                        val = (
                            c0 * G[ji, k, pl.ds(b, 8), :] + c1 * G[ji, k, pl.ds(b - sy, 8), :]
                        ) + (c2 * G[ji, k, pl.ds(b - 2 * sy, 8), :] + c3 * G[ji, k, pl.ds(b + sy, 8), :])
                        A[ji, rows, cols] = val
                        r.append(val)
                    p = [r[4 + i] + r[3 - i] for i in range(4)]
                    d = [r[4 + i] - r[3 - i] for i in range(4)]
                    s = [0.125 + 0.25 * i for i in range(4)]
                    L0 = (p[0] + p[1]) + (p[2] + p[3])
                    L1 = (s[0] * d[0] + s[1] * d[1]) + (s[2] * d[2] + s[3] * d[3])
                    L2 = (s[0] ** 2 * p[0] + s[1] ** 2 * p[1]) + (s[2] ** 2 * p[2] + s[3] ** 2 * p[3])
                    L3 = (s[0] ** 3 * d[0] + s[1] ** 3 * d[1]) + (s[2] ** 3 * d[2] + s[3] ** 3 * d[3])
                    M1 = L1 + mid * L0
                    M2 = L2 + mid * (L1 + M1)
                    M3 = L3 + mid * (3.0 * L2 + mid * (3.0 * L1 + mid * L0))
                    M.append((L0, M1, M2, M3))
                (a0, a1, a2, a3), (b0, b1, b2, b3) = M
                ya, yb = cy
                ya0, yb0 = ya * a0, yb * b0
                ya1, yb1 = ya * a1, yb * b1
                sums = [
                    a0 + b0,
                    a1 + b1,
                    ya0 + yb0,
                    a2 + b2,
                    ya1 + yb1,
                    ya * ya0 + yb * yb0,
                    (a3 + b3) + (ya * ya1 + yb * yb1),
                    ya * (a2 + ya * ya0) + yb * (b2 + yb * yb0),
                ]
                for m in range(8):
                    MO[n, group, k // 4, tt, k % 4, pl.ds(m, 8, stride=8), :] = sums[m]

        def core_copy(group):
            return pltpu.make_async_remote_copy(
                src_ref=MO.at[n, group, other], dst_ref=R1.at[n, group],
                send_sem=c_sem.at[n, group, 0], recv_sem=c_sem.at[n, group, 1],
                device_id=core_dev, device_id_type=MESH,
            )

        def scatter(group):
            core_copy(group).wait()

            @pl.loop(0, 4)
            def _(kk):
                for r in range(8):
                    rows = pl.ds(8 * r, 8)
                    for tt in range(2):
                        S[n, group, kk * 8 + r, tt] = MO[n, group, c, tt, kk, rows, :] + R1[n, group, tt, kk, rows, :]

            for d, (dev, q) in enumerate(chips):
                pltpu.make_async_remote_copy(
                    src_ref=S.at[n, group, q], dst_ref=R2.at[n, group, d],
                    send_sem=rs_sem.at[n, group, 0], recv_sem=rs_sem.at[n, group, 1],
                    device_id=dev, device_id_type=MESH,
                ).start()

        def piece(q):
            return pl.ds(pl.multiple_of(q * 16, 16), 12)

        def gather(group):
            total_wait(R2.at[n, group], rs_sem.at[n, group, 1])
            parts = [S[n, group, q_me]] + [R2[n, group, d] for d in range(CHIPS - 1)]
            while len(parts) > 1:
                parts = [a + b for a, b in zip(parts[::2], parts[1::2])]
            T4[...] = parts[0].reshape(16, 128)
            s = [T4[pl.ds(m, 2, stride=8), :] * 0.0625 for m in range(8)]
            rho = s[0]
            inv = 1.0 / rho
            ux, uy = s[1] * inv, s[2] * inv
            energy = s[3] + s[5]
            uu = ux * ux + uy * uy
            temp = jnp.maximum(energy * inv - uu, FLOOR)
            qx = 0.5 * (s[6] - 2.0 * (ux * s[3] + uy * s[4]) - ux * energy + 2.0 * rho * uu * ux)
            qy = 0.5 * (s[7] - 2.0 * (ux * s[4] + uy * s[5]) - uy * energy + 2.0 * rho * uu * uy)
            cold = 1.0 / temp
            scale = (4.0 * (1.0 - PRANDTL)) * inv * cold * cold
            fields = jnp.concatenate([rho, ux, uy, cold, scale * qx, scale * qy], axis=0)
            FO[n, group] = fields
            FB[n, c, group, piece(q_me)] = fields
            for dev, _ in chips:
                pltpu.make_async_remote_copy(
                    src_ref=FO.at[n, group], dst_ref=FB.at[n, c, group, piece(q_me)],
                    send_sem=ag_sem.at[n, group, 0], recv_sem=ag_sem.at[n, group, 1],
                    device_id=dev, device_id_type=MESH,
                ).start()

        def back_copy(group):
            return pltpu.make_async_remote_copy(
                src_ref=FB.at[n, c, group], dst_ref=FB.at[n, c, group],
                send_sem=d_sem.at[n, group, 0], recv_sem=d_sem.at[n, group, 1],
                device_id=core_dev, device_id_type=MESH,
            )

        def all_pieces(group):
            return FB.at[n, c, group, pl.ds(0, (CHIPS - 1) * 12)]

        def relax(group):
            @pl.loop(0, 2 * CHUNKS)
            def _(it):
                tt, k = it // CHUNKS, it % CHUNKS
                rows, cols = block(tile(group, tt), k)
                first = (k % 4) * 128 + tt
                rho, ux, uy, cold, bx, by = [
                    FB[n, k // 4, group, pl.ds(first + 2 * m, 8, stride=16), :] for m in range(6)
                ]
                keep = jnp.exp((-DT / TAU0) * rho * lax.rsqrt(cold))
                gp = rho * cold * (1.0 / math.pi) * (1.0 - keep)
                ax, ex, bxi = [], [], []
                for i in range(LX):
                    xi = speed(cx0 + i) - ux
                    a = xi * xi * cold
                    ax.append(a)
                    ex.append(jnp.exp(-a))
                    bxi.append(bx * xi)
                for j in range(LY):
                    yj = cy[j] - uy
                    ay = yj * yj * cold
                    ey = gp * jnp.exp(-ay)
                    ay = ay - 2.0
                    bj = by * yj
                    for i in range(LX):
                        ji = j * LX + i
                        shakhov = ex[i] * ey * (1.0 + (bxi[i] + bj) * (ax[i] + ay))
                        A[ji, rows, cols] = A[ji, rows, cols] * keep + shakhov

        sweep(0)
        core_copy(0).start()
        scatter(0)
        for m in mirrors:
            m.wait()
        sweep(1)
        core_copy(1).start()
        scatter(1)
        gather(0)
        gather(1)
        for group in range(2):
            total_wait(all_pieces(group), ag_sem.at[n, group, 1])
            back_copy(group).start()
        for group in range(2):
            back_copy(group).wait()
            relax(group)
        for group in range(2):
            total_wait(R2.at[n, group], rs_sem.at[n, group, 0])
            total_wait(all_pieces(group), ag_sem.at[n, group, 0])
        return 0

    lax.fori_loop(0, STEPS, step, 0)


def on_device(populations):
    shape = (LV, ROWS, CHUNKS * 128)
    dma = pltpu.SemaphoreType.DMA
    out = pl.pallas_call(
        kernel,
        out_shape=pltpu.VMEM(shape, F32),
        in_specs=[pl.BlockSpec(memory_space=pltpu.HBM)],
        out_specs=pl.BlockSpec(memory_space=pltpu.VMEM),
        scratch_shapes=[
            pltpu.SMEM((LX, 4), F32),
            pltpu.VMEM((LV, CHUNKS, PAD, 128), F32),
            pltpu.VMEM((STEPS, 2, 8, 128), F32),
            pltpu.VMEM((STEPS, 2, 8, 128), F32),
            pltpu.VMEM((LV * TILES, 8, 128), F32),
            pltpu.VMEM((STEPS, 2, 2, 2, 4, 64, 128), F32),
            pltpu.VMEM((STEPS, 2, 2, 4, 64, 128), F32),
            pltpu.VMEM((STEPS, 2, CHIPS, 2, 8, 128), F32),
            pltpu.VMEM((STEPS, 2, CHIPS - 1, 2, 8, 128), F32),
            pltpu.VMEM((16, 128), F32),
            pltpu.VMEM((STEPS, 2, 12, 128), F32),
            pltpu.VMEM((STEPS, 2, 2, CHIPS * 16, 128), F32),
            dma,
            dma((STEPS, 2)),
            dma((STEPS, 2, 6)),
            dma((STEPS, 2, 2)),
            dma((STEPS, 2, 2)),
            dma((STEPS, 2, 2)),
            dma((STEPS, 2, 2)),
        ],
        compiler_params=pltpu.CompilerParams(
            collective_id=0, has_side_effects=True, vmem_limit_bytes=24 << 20
        ),
        cost_estimate=pl.CostEstimate(flops=60 << 20, bytes_accessed=4 << 20, transcendentals=1 << 20),
    )(populations.reshape(shape))
    return out.reshape(populations.shape)


def solution(mesh):
    return jax.shard_map(
        on_device,
        mesh=mesh,
        in_specs=(P("vy", "vx", None, "gx"),),
        out_specs=P("vy", "vx", None, "gx"),
        check_vma=False,
    )
```

time: 1420 us -> 72.6 us (0.05)
  waiting for transfers between devices: 1330 us -> 0 us
  Pallas kernels: 0 us -> 69.5 us
  other arithmetic: 27.7 us -> 0 us
  starting transfers between devices: 18.5 us -> 0 us
    psum x2 -> x0, waiting for transfers between devices: 1280 us -> none  [advance_once(): totals = lax.psum(sums, ('vy', 'vx'))]
    pallas_call x0 -> x1, Pallas kernels: none -> 69.5 us  [on_device(): pl.pallas_call(kernel, out_shape=pltpu.VMEM(shape, F32), in_specs=[pl.Blo...]
    ppermute x12 -> x0, waiting for transfers between devices: 57.8 us -> none  [the longest x8 40.8 us: partner_2(): lax.ppermute(x, axis, [(i, i ^ 1 << stride) for i in range(lax.axis_size(...]
    sub x4 -> x0, other arithmetic: 19.7 us -> none  [upwind(): centre - 0.5 * courant * (plus_one - minus_one)]
    ppermute x12 -> x0, starting transfers between devices: 18.5 us -> none  [the longest x8 14.6 us: partner_2(): lax.ppermute(x, axis, [(i, i ^ 1 << stride) for i in range(lax.axis_size(...]
  transfers between devices with their start and end apart: 14 -> 0, of which waited for: 14 -> 0; matrix products, arithmetic and copies ran while one was open for 0% -> 0% of each run, Pallas kernels for 0% -> 0%
where the time goes in v2:
time: 72.6 us; the launch traced here: 72.4 us
  Pallas kernels  69.5 us (96%)
  local copies, waits for them, and re-layouts  2.91 us (4%)
    pallas_call x1, Pallas kernels, on_device(): pl.pallas_call(kernel, out_shape=pltpu.VMEM(shape, F32), in_specs=[pl.Blo...  69.5 us
    unnamed x3, local copies, waits for them, and re-layouts  2.91 us

profile of v2, /device:TPU:1, one launch (start us, length us, event | category | flops | bytes accessed | tf_op | source)
XLA Modules:
  0.0 72.4 jit_solution(13881716126894123580)
XLA Ops:
  0.0 0.0 copy-start
  0.0 1.6 %copy-done = f32[2,8,32,1024]{3,2,1,0:T(8,128)S(1)} copy-done((f32[2,8,32,1024]{3,2,1,0:T(8,128)S(1)}, f32[2,8,32,1024]{3,2,1,0:T(8,128)}, u32[]{:S(2)}) %copy-start) | copy-done | bytes 2097176
  1.6 69.5 %shard_map.17 = f32[16,32,1024]{2,1,0:T(8,128)S(1)} custom-call(f32[16,32,1024]{2,1,0:T(8,128)S(1)} %bitcast.3), custom_call_target="tpu_custom_call" | custom-call | flops 62914560 | bytes 4194304 | tf_op jit(solution)/shard_map/pallas_call | solution.py:322
  71.1 1.3 %copy.3 = f32[2,8,32,1024]{3,2,1,0:T(8,128)} copy(f32[2,8,32,1024]{3,2,1,0:T(8,128)S(1)} %bitcast.2) | data formatting | bytes 4194304
Async XLA Ops:
  0.0 1.6 %copy-start = (f32[2,8,32,1024]{3,2,1,0:T(8,128)S(1)}, f32[2,8,32,1024]{3,2,1,0:T(8,128)}, u32[]{:S(2)}) copy-start(f32[2,8,32,1024]{3,2,1,0:T(8,128)} %param.1) | copy-start | bytes 6291460

commit v3 on v2

v3 whole, which is shorter than its diff:
```python
import math

import jax
import jax.numpy as jnp
from jax import lax
from jax.experimental import pallas as pl
from jax.experimental.pallas import tpu as pltpu
from jax.sharding import PartitionSpec as P

STEPS = 2
DT = 0.125
TAU0 = 16.0
PRANDTL = 2.0 / 3.0
FLOOR = 1.0
MESH = pl.DeviceIdType.MESH
F32 = jnp.float32

LY, LX, ROWS, CHUNKS, TILES = 2, 8, 32, 8, 4
LV = LY * LX
PAD = 48
CHIPS = 32
FAR_FIRST = sorted(
    ((a, b, e) for a in range(4) for b in range(4) for e in range(2) if a or b or e),
    key=lambda t: -(min(t[0], 4 - t[0]) + min(t[1], 4 - t[1]) + 2 * t[2]),
)


def speed(index):
    return (index.astype(F32) + 0.5) * 0.25 - 4.0


def taps(nu):
    a = jnp.abs(nu)
    e = a * (1.0 - a * a) * (1.0 / 6.0)
    h = 0.5 * a
    s = 0.5 * a * a
    return 1.0 - 2.0 * s + 3.0 * e, h + s - 3.0 * e, e, s - h - e


def total_wait(ref, sem):
    pltpu.make_async_copy(ref, ref, sem).wait()


def kernel(
    x_hbm, A, TX, G, GH, HS, HR, HX, MO, R1, S, R2, T4, FO, FB,
    in_sem, h_sem, w_sem, c_sem, rs_sem, ag_sem, d_sem,
):
    g, v, x = lax.axis_index("gx"), lax.axis_index("vy"), lax.axis_index("vx")
    z, yh, c = v // 4, (v // 2) % 2, v % 2
    other = 1 - c
    q_me = (x * 4 + z) * 2 + yh
    core_dev = (g, v + 1 - 2 * c, x)
    gx_dev = (1 - g, v, x)
    mirror_dev = (g, 15 - v, x)
    chips = []
    for dx, dz, dy in FAR_FIRST:
        xx, zz, yy = (x + dx) % 4, (z + dz) % 4, (yh + dy) % 2
        chips.append(((g, zz * 4 + yy * 2 + c, xx), (xx * 4 + zz) * 2 + yy))

    load = pltpu.make_async_copy(x_hbm, A, in_sem)
    load.start()
    @pl.loop(0, LV)
    def _(ji):
        for k in range(CHUNKS):
            G[ji, k, 0:8, :] = jnp.zeros((8, 128), F32)
            G[ji, k, 40:48, :] = jnp.zeros((8, 128), F32)
        for n in range(STEPS):
            for r in range(4):
                GH[n, r, ji] = jnp.zeros((8, 128), F32)

    barrier = pltpu.get_barrier_semaphore()
    for d in (core_dev, gx_dev, mirror_dev):
        pl.semaphore_signal(barrier, inc=1, device_id=d, device_id_type=MESH)
    for d, _ in chips:
        pl.semaphore_signal(barrier, inc=1, device_id=d, device_id_type=MESH)

    cx0 = x * LX
    for i in range(LX):
        for m, tap in enumerate(taps(DT * speed(cx0 + i))):
            TX[i, m] = tap
    lane = lax.broadcasted_iota(jnp.int32, (8, 128), 1)
    right = x >= 2
    up = v >= 8
    sy = jnp.where(up, 1, -1)
    sub = lax.broadcasted_iota(jnp.int32, (8, 128), 0)
    send0 = jnp.where(up, 1, 0)
    cy = [speed(v * LY + j) for j in range(LY)]
    cy_taps = [taps(DT * s) for s in cy]
    mid = speed(cx0 + 3) + 0.125

    pl.semaphore_wait(barrier, CHIPS - 1 + 3)

    load.wait()

    def rows_of(*pairs):
        out = jnp.zeros((8, 128), F32)
        for row, value in pairs:
            out = jnp.where(sub == row, value, out)
        return out

    reflect = []
    inward = []
    for j in range(LY):
        _, c1, c2, c3 = cy_taps[j]
        near, far = jnp.where(up, c3, c1), jnp.where(up, c1, c3)
        second, first = jnp.where(up, 0.0, c2), jnp.where(up, c2, 0.0)
        reflect.append((
            (rows_of((0, near)), rows_of((0, second)), rows_of((1, second))),
            (rows_of((7, far)), rows_of((6, first)), rows_of((7, first))),
        ))
        inward.append((
            (rows_of((0, first)), rows_of((0, far), (1, first))),
            (rows_of((7, near), (6, second)), rows_of((7, second))),
        ))

    def tile(group, tt):
        return 1 + tt if group == 0 else 3 * tt

    def block(t, k):
        return pl.ds(pl.multiple_of(8 * t, 8), 8), pl.ds(pl.multiple_of(128 * k, 128), 128)

    def step(n, _):
        halos = []
        for part in range(2):
            acc = jnp.zeros((8, 128), F32)
            for p in range(32):
                ji, t = (part * 32 + p) // TILES, p % TILES
                ends = jnp.where(lane < 64, A[ji, 8 * t : 8 * t + 8, :128], A[ji, 8 * t : 8 * t + 8, 896:])
                ends = pltpu.roll(ends, (4 * p + 2) % 128, 1)
                acc = jnp.where((lane >= 4 * p) & (lane < 4 * p + 4), ends, acc)
            HS[n, part] = acc
            halos.append(pltpu.make_async_remote_copy(
                src_ref=HS.at[n, part], dst_ref=HR.at[n, part],
                send_sem=h_sem.at[n, 0, part], recv_sem=h_sem.at[n, 1, part],
                device_id=gx_dev, device_id_type=MESH,
            ))
            halos[-1].start()

        def unpack():
            def place(toward_right):
                for part in range(2):
                    ends = HR[n, part]
                    for p in range(32):
                        for m, shift in enumerate((1, 2, 127) if toward_right else (127, 126, 1)):
                            HX[m, part * 32 + p] = pltpu.roll(ends, (126 - 4 * p + shift) % 128, 1)

            pl.when(right)(lambda: place(True))
            pl.when(jnp.logical_not(right))(lambda: place(False))

        def stream(toward_right, tiles, flow):
            edge = lane if toward_right else 127 - lane
            masks = (edge < 1, edge < 2, edge > 126)
            shifts = (1, 2, 127) if toward_right else (127, 126, 1)

            @pl.loop(0, LX)
            def _(i):
                c0, c1, c2, c3 = [TX[i, m] for m in range(4)]
                for j, t in [(j, t) for j in range(LY) for t in tiles]:
                    ji = j * LX + i
                    memo = {}

                    def chunk(f):
                        k = f if toward_right else CHUNKS - 1 - f
                        return A[ji, 8 * t : 8 * t + 8, 128 * k : 128 * k + 128]

                    def rolled(m, f):
                        if (m, f) not in memo:
                            if 0 <= f < CHUNKS:
                                memo[m, f] = pltpu.roll(chunk(f), shifts[m], 1)
                            else:
                                memo[m, f] = HX[m, ji * TILES + t]
                        return memo[m, f]

                    for f in flow:
                        u1 = jnp.where(masks[0], rolled(0, f - 1), rolled(0, f))
                        u2 = jnp.where(masks[1], rolled(1, f - 1), rolled(1, f))
                        d1 = jnp.where(masks[2], rolled(2, f + 1), rolled(2, f))
                        out = (c0 * chunk(f) + c1 * u1) + (c2 * u2 + c3 * d1)
                        k = f if toward_right else CHUNKS - 1 - f
                        G[ji, k, pl.ds(8 + 8 * t, 8), :] = out

        def stream_tiles(tiles, flow):
            pl.when(right)(lambda: stream(True, tiles, flow))
            pl.when(jnp.logical_not(right))(lambda: stream(False, tiles, flow))

        stream_tiles(range(TILES), range(1, CHUNKS - 1))
        for h in halos:
            h.wait()
        unpack()
        stream_tiles(range(TILES), (0, CHUNKS - 1))

        mirrors = []
        for j in range(LY):
            for r in range(3):
                e = r + send0
                row = jnp.where(e < 2, 1 - e, 33 - e) + 8
                mirrors.append(pltpu.make_async_remote_copy(
                    src_ref=G.at[pl.ds(j * LX, LX), :, row, :],
                    dst_ref=GH.at[n, e, pl.ds((1 - j) * LX, LX)],
                    send_sem=w_sem.at[n, 0, j * 3 + r], recv_sem=w_sem.at[n, 1, j * 3 + r],
                    device_id=mirror_dev, device_id_type=MESH,
                ))
        for m in mirrors:
            m.start()

        def add_ghosts():
            @pl.loop(0, LX)
            def _(i):
                for j in range(LY):
                    ji = j * LX + i
                    for tt in range(2):
                        wa, wb = inward[j][tt]
                        rows = slice(24 * tt, 24 * tt + 8)
                        for k in range(CHUNKS):
                            cols = slice(128 * k, 128 * k + 128)
                            A[ji, rows, cols] = A[ji, rows, cols] + (
                                wa * GH[n, 2 * tt, ji, pl.ds(k, 1), :] + wb * GH[n, 2 * tt + 1, ji, pl.ds(k, 1), :]
                            )

        def along_x(r):
            p = [r[4 + i] + r[3 - i] for i in range(4)]
            d = [r[4 + i] - r[3 - i] for i in range(4)]
            s = [0.125 + 0.25 * i for i in range(4)]
            L0 = (p[0] + p[1]) + (p[2] + p[3])
            L1 = (s[0] * d[0] + s[1] * d[1]) + (s[2] * d[2] + s[3] * d[3])
            L2 = (s[0] ** 2 * p[0] + s[1] ** 2 * p[1]) + (s[2] ** 2 * p[2] + s[3] ** 2 * p[3])
            L3 = (s[0] ** 3 * d[0] + s[1] ** 3 * d[1]) + (s[2] ** 3 * d[2] + s[3] ** 3 * d[3])
            M1 = L1 + mid * L0
            M2 = L2 + mid * (L1 + M1)
            M3 = L3 + mid * (3.0 * L2 + mid * (3.0 * L1 + mid * L0))
            return L0, M1, M2, M3

        def sweep(group):
            @pl.loop(0, CHUNKS)
            def _(k):
              for tt in range(2):
                t = tile(group, tt)
                b = 8 + 8 * t
                rows, cols = block(t, k)
                even, odd = [], []
                for j in range(LY):
                    c0, c1, c2, c3 = cy_taps[j]
                    r, centres = [], []
                    for i in range(LX):
                        ji = j * LX + i
                        centre = G[ji, k, pl.ds(b, 8), :]
                        val = (c0 * centre + c1 * G[ji, k, pl.ds(b - sy, 8), :]) + (
                            c2 * G[ji, k, pl.ds(b - 2 * sy, 8), :] + c3 * G[ji, k, pl.ds(b + sy, 8), :]
                        )
                        A[ji, rows, cols] = val
                        r.append(val)
                        centres.append(centre)
                    M = along_x(r)
                    if group == 0:
                        even.append(M)
                        odd.append(M)
                    else:
                        wa, wb, wc = reflect[j][tt]
                        X = [
                            (wa * m + wb * pltpu.roll(m, 7, 0)) + wc * pltpu.roll(m, 1, 0) for m in along_x(centres)
                        ]
                        even.append([m + e for m, e in zip(M, X)])
                        odd.append([m - e for m, e in zip(M, X)])
                (a0, a1, a2, a3), (b0, b1, b2, b3) = even
                (d0, d1, d2, _), (e0, e1, e2, _) = odd
                ya, yb = cy
                yya, yyb = ya * ya, yb * yb
                sums = [
                    a0 + b0,
                    a1 + b1,
                    ya * d0 + yb * e0,
                    a2 + b2,
                    ya * d1 + yb * e1,
                    yya * a0 + yyb * b0,
                    (a3 + b3) + (yya * a1 + yyb * b1),
                    ya * (d2 + yya * d0) + yb * (e2 + yyb * e0),
                ]
                for m in range(8):
                    MO[n, group, k // 4, tt, k % 4, pl.ds(m, 8, stride=8), :] = sums[m]

        def core_copy(group):
            return pltpu.make_async_remote_copy(
                src_ref=MO.at[n, group, other], dst_ref=R1.at[n, group],
                send_sem=c_sem.at[n, group, 0], recv_sem=c_sem.at[n, group, 1],
                device_id=core_dev, device_id_type=MESH,
            )

        def scatter(group):
            core_copy(group).wait()

            @pl.loop(0, 4)
            def _(kk):
                for r in range(8):
                    rows = pl.ds(8 * r, 8)
                    for tt in range(2):
                        S[n, group, kk * 8 + r, tt] = MO[n, group, c, tt, kk, rows, :] + R1[n, group, tt, kk, rows, :]

            for d, (dev, q) in enumerate(chips):
                pltpu.make_async_remote_copy(
                    src_ref=S.at[n, group, q], dst_ref=R2.at[n, group, d],
                    send_sem=rs_sem.at[n, group, 0], recv_sem=rs_sem.at[n, group, 1],
                    device_id=dev, device_id_type=MESH,
                ).start()

        def piece(q):
            return pl.ds(pl.multiple_of(q * 16, 16), 12)

        def gather(group):
            total_wait(R2.at[n, group], rs_sem.at[n, group, 1])
            parts = [S[n, group, q_me]] + [R2[n, group, d] for d in range(CHIPS - 1)]
            while len(parts) > 1:
                parts = [a + b for a, b in zip(parts[::2], parts[1::2])]
            T4[...] = parts[0].reshape(16, 128)
            s = [T4[pl.ds(m, 2, stride=8), :] * 0.0625 for m in range(8)]
            rho = s[0]
            inv = 1.0 / rho
            ux, uy = s[1] * inv, s[2] * inv
            energy = s[3] + s[5]
            uu = ux * ux + uy * uy
            temp = jnp.maximum(energy * inv - uu, FLOOR)
            qx = 0.5 * (s[6] - 2.0 * (ux * s[3] + uy * s[4]) - ux * energy + 2.0 * rho * uu * ux)
            qy = 0.5 * (s[7] - 2.0 * (ux * s[4] + uy * s[5]) - uy * energy + 2.0 * rho * uu * uy)
            cold = 1.0 / temp
            scale = (4.0 * (1.0 - PRANDTL)) * inv * cold * cold
            fields = jnp.concatenate([rho, ux, uy, cold, scale * qx, scale * qy], axis=0)
            FO[n, group] = fields
            FB[n, c, group, piece(q_me)] = fields
            for dev, _ in chips:
                pltpu.make_async_remote_copy(
                    src_ref=FO.at[n, group], dst_ref=FB.at[n, c, group, piece(q_me)],
                    send_sem=ag_sem.at[n, group, 0], recv_sem=ag_sem.at[n, group, 1],
                    device_id=dev, device_id_type=MESH,
                ).start()

        def back_copy(group):
            return pltpu.make_async_remote_copy(
                src_ref=FB.at[n, c, group], dst_ref=FB.at[n, c, group],
                send_sem=d_sem.at[n, group, 0], recv_sem=d_sem.at[n, group, 1],
                device_id=core_dev, device_id_type=MESH,
            )

        def all_pieces(group):
            return FB.at[n, c, group, pl.ds(0, (CHIPS - 1) * 12)]

        def relax(group):
            @pl.loop(0, CHUNKS)
            def _(k):
                first = (k % 4) * 128

                def one(values, speeds, at):
                    rho, ux, uy, cold, bx, by = values
                    keep = jnp.exp((-DT / TAU0) * rho * lax.rsqrt(cold))
                    gp = rho * cold * (1.0 / math.pi) * (1.0 - keep)
                    ax, ex, bxi = [], [], []
                    for i in range(LX):
                        xi = speed(cx0 + i) - ux
                        a = xi * xi * cold
                        ax.append(a)
                        ex.append(jnp.exp(-a))
                        bxi.append(bx * xi)
                    for j in range(LY):
                        yj = speeds[j] - uy
                        ay = yj * yj * cold
                        ey = gp * jnp.exp(-ay)
                        ay = ay - 2.0
                        bj = by * yj
                        for i in range(LX):
                            ref, rows, cols = at(j * LX + i)
                            shakhov = ex[i] * ey * (1.0 + (bxi[i] + bj) * (ax[i] + ay))
                            ref[rows, cols] = ref[rows, cols] * keep + shakhov

                fields = []
                for tt in range(2):
                    rows, cols = block(tile(group, tt), k)
                    fields.append([
                        FB[n, k // 4, group, pl.ds(first + tt + 2 * m, 8, stride=16), :] for m in range(6)
                    ])
                    one(fields[tt], cy, lambda ji: (A.at[ji], rows, cols))

        sweep(0)
        core_copy(0).start()
        sweep(1)
        core_copy(1).start()
        scatter(0)
        scatter(1)
        for m in mirrors:
            m.wait()
        add_ghosts()
        gather(0)
        gather(1)
        for group in range(2):
            total_wait(all_pieces(group), ag_sem.at[n, group, 1])
            back_copy(group).start()
        back_copy(0).wait()
        relax(0)

        back_copy(1).wait()
        relax(1)
        for group in range(2):
            total_wait(R2.at[n, group], rs_sem.at[n, group, 0])
            total_wait(all_pieces(group), ag_sem.at[n, group, 0])
        return 0

    lax.fori_loop(0, STEPS, step, 0)


def on_device(populations):
    shape = (LV, ROWS, CHUNKS * 128)
    dma = pltpu.SemaphoreType.DMA
    out = pl.pallas_call(
        kernel,
        out_shape=pltpu.VMEM(shape, F32),
        in_specs=[pl.BlockSpec(memory_space=pltpu.HBM)],
        out_specs=pl.BlockSpec(memory_space=pltpu.VMEM),
        scratch_shapes=[
            pltpu.SMEM((LX, 4), F32),
            pltpu.VMEM((LV, CHUNKS, PAD, 128), F32),
            pltpu.VMEM((STEPS, 4, LV, 8, 128), F32),
            pltpu.VMEM((STEPS, 2, 8, 128), F32),
            pltpu.VMEM((STEPS, 2, 8, 128), F32),
            pltpu.VMEM((3, LV * TILES, 8, 128), F32),
            pltpu.VMEM((STEPS, 2, 2, 2, 4, 64, 128), F32),
            pltpu.VMEM((STEPS, 2, 2, 4, 64, 128), F32),
            pltpu.VMEM((STEPS, 2, CHIPS, 2, 8, 128), F32),
            pltpu.VMEM((STEPS, 2, CHIPS - 1, 2, 8, 128), F32),
            pltpu.VMEM((16, 128), F32),
            pltpu.VMEM((STEPS, 2, 12, 128), F32),
            pltpu.VMEM((STEPS, 2, 2, CHIPS * 16, 128), F32),
            dma,
            dma((STEPS, 2, 2)),
            dma((STEPS, 2, 6)),
            dma((STEPS, 2, 2)),
            dma((STEPS, 2, 2)),
            dma((STEPS, 2, 2)),
            dma((STEPS, 2, 2)),
        ],
        compiler_params=pltpu.CompilerParams(
            collective_id=0, has_side_effects=True, vmem_limit_bytes=61 << 20
        ),
        cost_estimate=pl.CostEstimate(flops=60 << 20, bytes_accessed=4 << 20, transcendentals=1 << 20),
    )(populations.reshape(shape))
    return out.reshape(populations.shape)


def solution(mesh):
    return jax.shard_map(
        on_device,
        mesh=mesh,
        in_specs=(P("vy", "vx", None, "gx"),),
        out_specs=P("vy", "vx", None, "gx"),
        check_vma=False,
    )
```

time: 72.6 us -> 66.2 us (0.912)
  Pallas kernels: 69.5 us -> 64.8 us
  local copies, waits for them, and re-layouts: 2.91 us -> 1.32 us
    pallas_call x1, Pallas kernels: 69.5 us -> 64.8 us  [on_device(): pl.pallas_call(kernel, out_shape=pltpu.VMEM(shape, F32), in_specs=[pl.Blo...]
    unnamed x3 -> x1, local copies, waits for them, and re-layouts: 2.91 us -> 1.32 us
where the time goes in v3:
time: 66.2 us; the launch traced here: 66.1 us
  Pallas kernels  64.8 us (98%)
  local copies, waits for them, and re-layouts  1.32 us (2%)
    pallas_call x1, Pallas kernels, on_device(): pl.pallas_call(kernel, out_shape=pltpu.VMEM(shape, F32), in_specs=[pl.Blo...  64.8 us

profile of v3, /device:TPU:1, one launch (start us, length us, event | category | flops | bytes accessed | tf_op | source)
XLA Modules:
  0.0 66.1 jit_solution(1563125692326798123)
XLA Ops:
  0.0 64.8 %shard_map.17 = f32[16,32,1024]{2,1,0:T(8,128)S(1)} custom-call(f32[16,32,1024]{2,1,0:T(8,128)} %bitcast.3), custom_call_target="tpu_custom_call" | custom-call | flops 62914560 | bytes 4194304 | tf_op jit(solution)/shard_map/pallas_call | solution.py:410
  64.8 1.3 %copy.3 = f32[2,8,32,1024]{3,2,1,0:T(8,128)} copy(f32[2,8,32,1024]{3,2,1,0:T(8,128)S(1)} %bitcast.2) | data formatting | bytes 4194304

commit v4 on v3

--- a/solution.py
+++ b/solution.py
@@ -183,25 +183,29 @@
             pl.when(right)(lambda: stream(True, tiles, flow))
             pl.when(jnp.logical_not(right))(lambda: stream(False, tiles, flow))
 
+        def mirror(part, first, count):
+            copies = []
+            for j in range(LY):
+                for r in range(3):
+                    e = r + send0
+                    row = jnp.where(e < 2, 1 - e, 33 - e) + 8
+                    copies.append(pltpu.make_async_remote_copy(
+                        src_ref=G.at[pl.ds(j * LX, LX), pl.ds(first, count), row, :],
+                        dst_ref=GH.at[n, e, pl.ds((1 - j) * LX, LX), pl.ds(first, count)],
+                        send_sem=w_sem.at[n, 0, part * 6 + j * 3 + r], recv_sem=w_sem.at[n, 1, part * 6 + j * 3 + r],
+                        device_id=mirror_dev, device_id_type=MESH,
+                    ))
+            for m in copies:
+                m.start()
+            return copies
+
         stream_tiles(range(TILES), range(1, CHUNKS - 1))
+        mirrors = mirror(0, 1, CHUNKS - 2)
         for h in halos:
             h.wait()
         unpack()
         stream_tiles(range(TILES), (0, CHUNKS - 1))
-
-        mirrors = []
-        for j in range(LY):
-            for r in range(3):
-                e = r + send0
-                row = jnp.where(e < 2, 1 - e, 33 - e) + 8
-                mirrors.append(pltpu.make_async_remote_copy(
-                    src_ref=G.at[pl.ds(j * LX, LX), :, row, :],
-                    dst_ref=GH.at[n, e, pl.ds((1 - j) * LX, LX)],
-                    send_sem=w_sem.at[n, 0, j * 3 + r], recv_sem=w_sem.at[n, 1, j * 3 + r],
-                    device_id=mirror_dev, device_id_type=MESH,
-                ))
-        for m in mirrors:
-            m.start()
+        mirrors += mirror(1, 0, 1) + mirror(2, CHUNKS - 1, 1)
 
         def add_ghosts():
             @pl.loop(0, LX)
@@ -428,7 +432,7 @@
             pltpu.VMEM((STEPS, 2, 2, CHIPS * 16, 128), F32),
             dma,
             dma((STEPS, 2, 2)),
-            dma((STEPS, 2, 6)),
+            dma((STEPS, 2, 18)),
             dma((STEPS, 2, 2)),
             dma((STEPS, 2, 2)),
             dma((STEPS, 2, 2)),

time: 66.2 us -> 61.2 us (0.924)
  Pallas kernels: 64.8 us -> 59.4 us
    pallas_call x1, Pallas kernels: 64.8 us -> 59.4 us  [on_device(): pl.pallas_call(kernel, out_shape=pltpu.VMEM(shape, F32), in_specs=[pl.Blo...]
where the time goes in v4:
time: 61.2 us; the launch traced here: 60.7 us
  Pallas kernels  59.4 us (97%)
  local copies, waits for them, and re-layouts  1.32 us (2%)
    pallas_call x1, Pallas kernels, on_device(): pl.pallas_call(kernel, out_shape=pltpu.VMEM(shape, F32), in_specs=[pl.Blo...  59.4 us
    unnamed x1, local copies, waits for them, and re-layouts  1.32 us

profile of v4, /device:TPU:1, one launch (start us, length us, event | category | flops | bytes accessed | tf_op | source)
XLA Modules:
  0.0 60.7 jit_solution(2160009826846065730)
XLA Ops:
  0.0 59.4 %shard_map.17 = f32[16,32,1024]{2,1,0:T(8,128)S(1)} custom-call(f32[16,32,1024]{2,1,0:T(8,128)} %bitcast.3), custom_call_target="tpu_custom_call" | custom-call | flops 62914560 | bytes 4194304 | tf_op jit(solution)/shard_map/pallas_call | solution.py:414
  59.4 1.3 %copy.3 = f32[2,8,32,1024]{3,2,1,0:T(8,128)} copy(f32[2,8,32,1024]{3,2,1,0:T(8,128)S(1)} %bitcast.2) | data formatting | bytes 4194304

commit v5 on v4

--- a/solution.py
+++ b/solution.py
@@ -199,13 +199,15 @@
                 m.start()
             return copies
 
-        stream_tiles(range(TILES), range(1, CHUNKS - 1))
+        stream_tiles((0, 3), range(1, CHUNKS - 1))
         mirrors = mirror(0, 1, CHUNKS - 2)
+        stream_tiles((1, 2), range(1, CHUNKS - 1))
         for h in halos:
             h.wait()
         unpack()
-        stream_tiles(range(TILES), (0, CHUNKS - 1))
+        stream_tiles((0, 3), (0, CHUNKS - 1))
         mirrors += mirror(1, 0, 1) + mirror(2, CHUNKS - 1, 1)
+        stream_tiles((1, 2), (0, CHUNKS - 1))
 
         def add_ghosts():
             @pl.loop(0, LX)

time: 61.2 us -> 62 us (1.013)
  Pallas kernels: 59.4 us -> 60.6 us
    pallas_call x1, Pallas kernels: 59.4 us -> 60.6 us  [on_device(): pl.pallas_call(kernel, out_shape=pltpu.VMEM(shape, F32), in_specs=[pl.Blo...]
where the time goes in v5:
time: 62 us; the launch traced here: 61.9 us
  Pallas kernels  60.6 us (98%)
  local copies, waits for them, and re-layouts  1.32 us (2%)
    pallas_call x1, Pallas kernels, on_device(): pl.pallas_call(kernel, out_shape=pltpu.VMEM(shape, F32), in_specs=[pl.Blo...  60.6 us
    unnamed x1, local copies, waits for them, and re-layouts  1.32 us

profile of v5, /device:TPU:1, one launch (start us, length us, event | category | flops | bytes accessed | tf_op | source)
XLA Modules:
  0.0 61.9 jit_solution(14704529479070020631)
XLA Ops:
  0.0 60.6 %shard_map.17 = f32[16,32,1024]{2,1,0:T(8,128)S(1)} custom-call(f32[16,32,1024]{2,1,0:T(8,128)} %bitcast.3), custom_call_target="tpu_custom_call" | custom-call | flops 62914560 | bytes 4194304 | tf_op jit(solution)/shard_map/pallas_call | solution.py:416
  60.6 1.3 %copy.3 = f32[2,8,32,1024]{3,2,1,0:T(8,128)} copy(f32[2,8,32,1024]{3,2,1,0:T(8,128)S(1)} %bitcast.2) | data formatting | bytes 4194304
